TPU v7x, 32 devices: a whole 2x2x4 slice. The times are simulated.
32 devices in a mesh: dp: 4 (over z), seq: 8 (over y, x, core).
Axes of the slice: x: 2, y: 2, z: 4, core: 2. Of those that a mesh axis runs over, the one named last changes fastest.
Arguments:
- tokens: bfloat16 [4096, 2688], P(('dp', 'seq')), may hold values from -6 to 6
- q_weight: bfloat16 [2688, 4096], P('dp', 'seq'), may hold values from -0.125 to 0.125
- key_projection: bfloat16 [2688, 2048], P('dp', 'seq'), may hold values from -0.125 to 0.125
- value_projection: bfloat16 [2688, 2048], P('dp', 'seq'), may hold values from -0.125 to 0.125
- query_norm_gain: float32 [128], replicated, may hold values from 0.5 to 2.5
- key_norm_gain: float32 [128], replicated, may hold values from 0.5 to 2.5
- doc_lengths: int32 [4, 4], P('dp'), may hold values from 1 to 768, 1024 in all within a row
- out_cot: bfloat16 [4096, 4096], P('dp', 'seq'), may hold values from -6 to 6
Outputs:
- attn_out: bfloat16 [4096, 4096], P(('dp', 'seq'))
- token_grad: bfloat16 [4096, 2688], P(('dp', 'seq'))
- q_weight_grad: float32 [2688, 4096], P('dp', 'seq')
- k_weight_grad: float32 [2688, 2048], P('dp', 'seq')
- v_weight_grad: float32 [2688, 2048], P('dp', 'seq')
Inputs may be any that keep to these rules, and one draw needn't show every extreme that they name: `doc_lengths`: each row's 4 lengths add up to 1024, and in every row the longest document has exactly 768 tokens.
All inputs are finite; a program needn't handle non-finite values.
Results may differ from a plain program's by a relative error of at most 0.015.
Values may be sent and summed in bfloat16 or wider, within the bound.
No kernel may reach another device: no remote copies, remote signals or barrier semaphores. Data moves between devices by JAX's collectives and lax.ppermute only.
A program may use at most 128 MiB of HBM per device.

v0:
```python
import jax
import jax.numpy as jnp
from jax import lax
from jax.sharding import PartitionSpec as P

HEAD_WIDTH = 128
WINDOW = 1024


score_scale = 168.0 ** (-0.5)
rope_base = 10000.0
norm_eps = 1e-06


def doc_layout(length_row, length):
    ends = jnp.cumsum(length_row, dtype=jnp.int32)
    starts = ends - length_row
    token = jnp.arange(length, dtype=jnp.int32)
    doc_index = jnp.sum(
        (token[:, None] >= ends[None, :]).astype(jnp.int32), axis=1, dtype=jnp.int32
    )
    member = doc_index[:, None] == jnp.arange(length_row.shape[0], dtype=jnp.int32)[None, :]
    position = token - jnp.sum(jnp.where(member, starts[None, :], 0), axis=1, dtype=jnp.int32)
    return (doc_index, position)


def rope_tables(position, head_size):
    half = head_size // 2
    inverse = rope_base ** (-jnp.arange(half, dtype=jnp.float32) * (2.0 / head_size))
    angle = position.astype(jnp.float32)[:, None] * inverse[None, :]
    cosine = jnp.concatenate([jnp.cos(angle), jnp.cos(angle)], axis=1)
    sine = jnp.concatenate([jnp.sin(angle), jnp.sin(angle)], axis=1)
    return (cosine, sine)


def norm_rotate(vectors, gain, cosine, sine):
    factor = lax.rsqrt(jnp.mean(vectors * vectors, axis=-1, keepdims=True) + norm_eps)
    normed = vectors * factor * gain
    half = vectors.shape[-1] // 2
    turned = jnp.concatenate([-normed[..., half:], normed[..., :half]], axis=-1)
    return normed * cosine[:, None, :] + turned * sine[:, None, :]


def shape_heads(
    projected_rows,
    query_norm_gain,
    key_norm_gain,
    cosine,
    sine,
    query_heads,
    value_heads,
    head_size,
):
    length = projected_rows.shape[0]
    query_cols = query_heads * head_size
    key_columns = value_heads * head_size
    queries = projected_rows[:, :query_cols].reshape(length, query_heads, head_size)
    keys = projected_rows[:, query_cols : query_cols + key_columns].reshape(
        length, value_heads, head_size
    )
    values = projected_rows[:, query_cols + key_columns :].reshape(length, value_heads, head_size)
    return (
        norm_rotate(queries, query_norm_gain, cosine, sine),
        norm_rotate(keys, key_norm_gain, cosine, sine),
        values,
    )


def band_mask(doc_index, query_start, key_start, query_rows, key_rows):
    query_pos = query_start + jnp.arange(query_rows, dtype=jnp.int32)
    key_pos = key_start + jnp.arange(key_rows, dtype=jnp.int32)
    query_doc = lax.dynamic_slice_in_dim(doc_index, query_start, query_rows, 0)
    key_doc = lax.dynamic_slice_in_dim(doc_index, key_start, key_rows, 0)
    spacing = query_pos[:, None] - key_pos[None, :]
    return (query_doc[:, None] == key_doc[None, :]) & (spacing >= 0) & (spacing < WINDOW)


def block_probs(query_part, key_part, allowed):
    scores = (
        jnp.einsum("qhgd,khd->hgqk", query_part, key_part, preferred_element_type=jnp.float32)
        * score_scale
    )
    weights = jnp.where(allowed[None, None], jnp.exp(scores), 0.0)
    return weights / jnp.sum(weights, axis=-1, keepdims=True)


def layer_kernel(
    projected_rows, length_row, cotangent, query_norm_gain, key_norm_gain, query_heads, value_heads
):
    length = projected_rows.shape[0]
    doc_index, position = doc_layout(length_row, length)
    cosine, sine = rope_tables(position, HEAD_WIDTH)
    (queries, keys, values), pull = jax.vjp(
        lambda inner: shape_heads(
            inner,
            query_norm_gain,
            key_norm_gain,
            cosine,
            sine,
            query_heads,
            value_heads,
            HEAD_WIDTH,
        ),
        projected_rows,
    )
    group = query_heads // value_heads
    query_bf = queries.astype(jnp.bfloat16).reshape(length, value_heads, group, HEAD_WIDTH)
    key_bf = keys.astype(jnp.bfloat16)
    value_bf = values.astype(jnp.bfloat16)
    grad_out = cotangent.reshape(length, value_heads, group, HEAD_WIDTH)
    query_rows = min(512, length)
    key_rows = min(length, query_rows + WINDOW)
    blocks = length // query_rows

    def block_view(index):
        index = index.astype(jnp.int32)
        query_start = index * query_rows
        key_start = jnp.maximum(query_start + query_rows - key_rows, 0)
        query_part = lax.dynamic_slice_in_dim(query_bf, query_start, query_rows, 0)
        key_part = lax.dynamic_slice_in_dim(key_bf, key_start, key_rows, 0)
        value_part = lax.dynamic_slice_in_dim(value_bf, key_start, key_rows, 0)
        allowed = band_mask(doc_index, query_start, key_start, query_rows, key_rows)
        return (
            query_start,
            key_start,
            query_part,
            key_part,
            value_part,
            block_probs(query_part, key_part, allowed),
        )

    def forward_block(index):
        _, _, _, _, value_part, probs = block_view(index)
        mixed = jnp.einsum(
            "hgqk,khd->qhgd",
            probs.astype(jnp.bfloat16),
            value_part,
            preferred_element_type=jnp.float32,
        )
        return mixed.astype(jnp.bfloat16).reshape(query_rows, query_heads * HEAD_WIDTH)

    head_output = lax.map(forward_block, jnp.arange(blocks, dtype=jnp.int32)).reshape(
        length, query_heads * HEAD_WIDTH
    )

    def backward_block(index, carry):
        grad_query, grad_key, grad_value = carry
        query_start, key_start, query_part, key_part, value_part, probs = block_view(index)
        grad_part = lax.dynamic_slice_in_dim(grad_out, query_start, query_rows, 0)
        probs_bf = probs.astype(jnp.bfloat16)
        value_term = jnp.einsum(
            "hgqk,qhgd->khd", probs_bf, grad_part, preferred_element_type=jnp.float32
        )
        grad_probs = jnp.einsum(
            "qhgd,khd->hgqk", grad_part, value_part, preferred_element_type=jnp.float32
        )
        delta = jnp.sum(probs * grad_probs, axis=-1, keepdims=True)
        grad_scores = (probs * (grad_probs - delta)).astype(jnp.bfloat16)
        query_term = (
            jnp.einsum("hgqk,khd->qhgd", grad_scores, key_part, preferred_element_type=jnp.float32)
            * score_scale
        )
        key_term = (
            jnp.einsum(
                "hgqk,qhgd->khd", grad_scores, query_part, preferred_element_type=jnp.float32
            )
            * score_scale
        )
        grad_query = lax.dynamic_update_slice_in_dim(grad_query, query_term, query_start, 0)
        grad_key = lax.dynamic_update_slice_in_dim(
            grad_key,
            lax.dynamic_slice_in_dim(grad_key, key_start, key_rows, 0) + key_term,
            key_start,
            0,
        )
        grad_value = lax.dynamic_update_slice_in_dim(
            grad_value,
            lax.dynamic_slice_in_dim(grad_value, key_start, key_rows, 0) + value_term,
            key_start,
            0,
        )
        return (grad_query, grad_key, grad_value)

    start_grads = (
        jnp.zeros((length, value_heads, group, HEAD_WIDTH), jnp.float32),
        jnp.zeros((length, value_heads, HEAD_WIDTH), jnp.float32),
        jnp.zeros((length, value_heads, HEAD_WIDTH), jnp.float32),
    )
    grad_query, grad_key, grad_value = lax.fori_loop(0, blocks, backward_block, start_grads)
    (projection_gradient,) = pull(
        (grad_query.reshape(length, query_heads, HEAD_WIDTH), grad_key, grad_value)
    )
    return (head_output, projection_gradient.astype(jnp.bfloat16))


def local(
    tokens,
    q_weight,
    key_projection,
    value_projection,
    query_norm_gain,
    key_norm_gain,
    doc_lengths,
    out_cot,
):
    query_whole, key_whole, value_whole = (
        lax.all_gather(q_weight, "dp", axis=0, tiled=True),
        lax.all_gather(key_projection, "dp", axis=0, tiled=True),
        lax.all_gather(value_projection, "dp", axis=0, tiled=True),
    )
    joined = jnp.concatenate([query_whole, key_whole, value_whole], axis=1)
    query_heads = q_weight.shape[1] // HEAD_WIDTH
    value_heads = key_projection.shape[1] // HEAD_WIDTH
    row_tokens = lax.all_gather(tokens, "seq", axis=0, tiled=True)
    projected_rows = jnp.dot(row_tokens, joined, preferred_element_type=jnp.float32)
    head_output, projection_gradient = layer_kernel(
        projected_rows,
        doc_lengths[0],
        out_cot,
        query_norm_gain,
        key_norm_gain,
        query_heads,
        value_heads,
    )
    attn_out = lax.all_to_all(head_output, "seq", split_axis=0, concat_axis=1, tiled=True)
    token_grad = lax.psum_scatter(
        lax.dot_general(
            projection_gradient,
            joined,
            (((1,), (1,)), ((), ())),
            preferred_element_type=jnp.float32,
        ).astype(jnp.bfloat16),
        "seq",
        scatter_dimension=0,
        tiled=True,
    )
    weight_terms = lax.dot_general(
        row_tokens,
        projection_gradient,
        (((0,), (0,)), ((), ())),
        preferred_element_type=jnp.float32,
    )
    query_cols = q_weight.shape[1]
    key_columns = key_projection.shape[1]
    query_grad, key_grad, value_grad = (
        lax.psum_scatter(
            weight_terms[:, :query_cols].astype(jnp.bfloat16), "dp", scatter_dimension=0, tiled=True
        ).astype(jnp.float32),
        lax.psum_scatter(
            weight_terms[:, query_cols : query_cols + key_columns].astype(jnp.bfloat16),
            "dp",
            scatter_dimension=0,
            tiled=True,
        ).astype(jnp.float32),
        lax.psum_scatter(
            weight_terms[:, query_cols + key_columns :].astype(jnp.bfloat16),
            "dp",
            scatter_dimension=0,
            tiled=True,
        ).astype(jnp.float32),
    )
    return (attn_out, token_grad, query_grad, key_grad, value_grad)


def solution(mesh):
    placed = (
        P(("dp", "seq"), None),
        P("dp", "seq"),
        P("dp", "seq"),
        P("dp", "seq"),
        P(),
        P(),
        P("dp", None),
        P("dp", "seq"),
    )
    return jax.shard_map(
        local,
        mesh=mesh,
        in_specs=placed,
        out_specs=(
            P(("dp", "seq"), None),
            P(("dp", "seq"), None),
            P("dp", "seq"),
            P("dp", "seq"),
            P("dp", "seq"),
        ),
        check_vma=False,
    )
```

profile of v0, /device:TPU:0, one launch (start us, length us, event | category | flops | bytes accessed | tf_op | source)
XLA Modules:
  0.0 478.8 jit_solution(16337218059402013264)
XLA Ops:
  16.3 53.0 %all-gather.5.cloned.1.call-done = bf16[2688,512]{1,0:T(8,128)(2,1)} async-done(((bf16[672,512]{1,0:T(8,128)(2,1)}), bf16[2688,512]{1,0:T(8,128)(2,1)}) %all-gather.5.cloned.1.call-update) | async-done | bytes 2752528 | tf_op jit(solution)/shard_map/all_gather | solution.py:207
  69.3 3.6 constant_dynamic-update-slice_fusion.3
  72.9 30.6 %all-gather.7.cloned.1.call-done = bf16[2688,256]{1,0:T(8,128)(2,1)} async-done(((bf16[672,256]{1,0:T(8,128)(2,1)}), bf16[2688,256]{1,0:T(8,128)(2,1)}) %all-gather.7.cloned.1.call-update) | async-done | bytes 1376272 | tf_op jit(solution)/shard_map/all_gather | solution.py:208
  103.5 2.6 constant_dynamic-update-slice_fusion.2
  106.0 31.8 %all-gather.9.cloned.1.call-done = bf16[2688,256]{1,0:T(8,128)(2,1)} async-done(((bf16[672,256]{1,0:T(8,128)(2,1)}), bf16[2688,256]{1,0:T(8,128)(2,1)}) %all-gather.9.cloned.1.call-update) | async-done | bytes 1376272 | tf_op jit(solution)/shard_map/all_gather | solution.py:209
  137.8 2.6 constant_dynamic-update-slice_fusion.1
  140.4 40.3 %all-gather.11.cloned.1.call-done = bf16[1024,2688]{1,0:T(8,128)(2,1)} async-done(((bf16[128,2688]{1,0:T(8,128)(2,1)}), bf16[1024,2688]{1,0:T(8,128)(2,1)}) %all-gather.11.cloned.1.call-update) | async-done | bytes 5505040 | tf_op jit(solution)/shard_map/all_gather | solution.py:214
  180.7 9.8 %convolution_bitcast_fusion.1 = f32[1024,1024]{0,1:T(8,128)S(1)} fusion(bf16[2688,1024]{1,0:T(8,128)(2,1)} %constant_dynamic-update-slice_fusion.1, bf16[1024,2688]{1,0:T(8,128)(2,1)} %all-gather.11.cloned.1.call-done), kind=kOutput, calls=%fused_computation.63 | convolution fusion | flops 5637144576 | bytes 15204352 | tf_op jit(solution)/shard_map/dot_general | solution.py:215
  197.7 3.3 copy.90
  201.0 3.2 copy.91
  207.4 4.5 fusion.48
  213.5 49.2 %while.37 = (s32[]{:T(128)}, f32[1024,2,2,128]{3,0,2,1:T(8,128)}, f32[1024,2,128]{0,2,1:T(8,128)S(1)}, f32[1024,2,128]{0,2,1:T(8,128)}, s32[1024]{0:T(1024)S(1)}...) while((s32[]{:T(128)}, f32[1024,2,2,128]{3,0,2,1:T(8,128)}, ...), condition=%wide.region_11.12_spmd.clone, body=%wide.region_8.11_spmd.clone.sunk | while | flops 2726819328 | bytes 162601312 | solution.py:189
  214.3 3.5 bitcast_reduce_fusion.5
  217.9 3.9 fusion.90
  228.5 3.5 fusion.93
  233.3 4.7 fusion.94
  238.8 3.5 bitcast_reduce_fusion.5
  242.3 3.9 fusion.90
  252.9 3.5 fusion.93
  257.7 5.0 %fusion.94 = f32[1024,2,128]{0,2,1:T(8,128)} fusion(f32[1024,2,128]{0,2,1:T(8,128)} %get-tuple-element.788, pred[]{:T(512)S(6)} %compare.10, bf16[1024,2,2,128]{0,3,2,1:T(8,128)(2,1)} %get-tuple-element.806, s32[]{:T(128)S(6)} %select_n.111, f32[2,512,2,1024]{3,1,2,0:T(8,128)S(1)} %copy-done.2, f32[2,2,512]{2,1,0:T(2,128)S(1)} %get-tuple-element.731, ...), kind=kOutput, calls=%fused_computation.42.clone.1 | convolution fusion | flops 545783808 | bytes 11542533 | tf_op jit(solution)/shard_map/while/body/eval_jaxpr/hgqk,qhgd->khd/dot_general | solution.py:151
  275.6 6.8 %fusion.46 = bf16[2688,1024]{0,1:T(8,128)(2,1)S(1)} fusion(bf16[1024,2688]{1,0:T(8,128)(2,1)S(1)} %bitcast.188, f32[1024,512]{0,1:T(8,128)S(1)} %bitcast.178, f32[1024,256]{0,1:T(8,128)S(1)} %bitcast.183, f32[1024,256]{0,1:T(8,128)S(1)} %bitcast.191), kind=kOutput, calls=%fused_computation.60 | convolution fusion | flops 5643042816 | bytes 15204352 | tf_op jit(solution)/shard_map/dot_general | solution.py:237
  286.1 2.5 copy.116
  290.3 3.6 slice.51
  293.9 4.9 %copy.114 = bf16[2688,512]{1,0:T(8,128)(2,1)} copy(bf16[2688,512]{0,1:T(8,128)(2,1)} %slice.51) | data formatting | bytes 5505024
  298.9 11.2 %convolution_convert_fusion.1 = bf16[1024,2688]{1,0:T(8,128)(2,1)} fusion(bf16[2688,1024]{1,0:T(8,128)(2,1)} %constant_dynamic-update-slice_fusion.1, f32[1024,512]{0,1:T(8,128)S(1)} %bitcast.179, f32[1024,256]{0,1:T(8,128)} %bitcast.182, f32[1024,256]{0,1:T(8,128)} %bitcast.190), kind=kOutput, calls=%fused_computation.59 | convolution fusion | flops 5643042816 | bytes 15204352 | tf_op jit(solution)/shard_map/dot_general | solution.py:227
  311.5 16.3 %while.36 = (s32[]{:T(128)}, bf16[2,512,512]{2,1,0:T(8,128)(2,1)}, s32[2]{0:T(128)S(1)}, s32[1024]{0:T(1024)S(1)}, bf16[1024,2,2,128]{3,0,2,1:T(8,128)(2,1)S(1)}...) while((s32[]{:T(128)}, bf16[2,512,512]{2,1,0:T(8,128)(2,1)}, ...), condition=%wide.region_7.8_spmd, body=%wide.region_5.7_spmd.sunk | while | flops 1091829248 | bytes 22584024 | solution.py:142
  313.5 2.5 bitcast_reduce_fusion.4
  321.7 2.5 bitcast_reduce_fusion.4
  327.8 18.8 %all_to_all.19 = bf16[8,128,512]{2,1,0:T(8,128)(2,1)S(1)} all-to-all(bf16[8,128,512]{2,1,0:T(8,128)(2,1)} %bitcast.185), channel_id=1, replica_groups=mesh['dp'=4,'seq'=8] {'seq'}, dimensions={0} | all-to-all | bytes 2097152 | tf_op jit(solution)/shard_map/all_to_all | solution.py:225
  350.7 4.3 reduce-scatter.17.cloned.1.call-done
  357.2 53.2 %reduce-scatter.13.cloned.1.call-done = bf16[672,512]{1,0:T(8,128)(2,1)} async-done(((bf16[2688,512]{1,0:T(8,128)(2,1)}), bf16[672,512]{1,0:T(8,128)(2,1)}) %reduce-scatter.13.cloned.1.call-update) | async-done | bytes 688144
  413.1 58.9 %reduce-scatter.11.cloned.1.call-done = bf16[128,2688]{1,0:T(8,128)(2,1)} async-done(((bf16[1024,2688]{1,0:T(8,128)(2,1)}), bf16[128,2688]{1,0:T(8,128)(2,1)}) %reduce-scatter.11.cloned.1.call-update) | async-done | bytes 688144 | tf_op jit(solution)/shard_map/reduce_scatter | solution.py:226
  (175 shorter events, 76.6 us)
Async XLA Ops:
  7.2 7.8 %copy-start.17 = (bf16[1024,512]{1,0:T(8,128)(2,1)S(1)}, bf16[1024,512]{1,0:T(8,128)(2,1)}, u32[]{:S(2)}) copy-start(bf16[1024,512]{1,0:T(8,128)(2,1)} %param.19) | copy-start | bytes 3145732
  7.2 62.1 %all-gather.5.cloned.1.call-start = ((), (), s32[]{:S(2)}) async-start(), calls=%async_computation.5 | async-start | bytes 3440640 | tf_op jit(solution)/shard_map/all_gather | solution.py:207
  7.9 95.5 %all-gather.7.cloned.1.call-start = ((), (), s32[]{:S(2)}) async-start(), calls=%async_computation.6 | async-start | bytes 1720320 | tf_op jit(solution)/shard_map/all_gather | solution.py:208
  8.7 129.2 %all-gather.9.cloned.1.call-start = ((), (), s32[]{:S(2)}) async-start(), calls=%async_computation.7 | async-start | bytes 1720320 | tf_op jit(solution)/shard_map/all_gather | solution.py:209
  9.4 171.4 %all-gather.11.cloned.1.call-start = ((), (), s32[]{:S(2)}) async-start(), calls=%async_computation.8 | async-start | bytes 6193152 | tf_op jit(solution)/shard_map/all_gather | solution.py:214
  10.0 338.6 %reduce-scatter.15.cloned.1.call-start = ((), (), s32[]{:S(2)}) async-start(), calls=%async_computation.11 | async-start | bytes 1720320
  12.8 179.7 %copy-start.6 = (f32[1024,128]{0,1:T(8,128)}, f32[1024,128]{0,1:T(8,128)S(1)}, u32[]{:S(2)}) copy-start(f32[1024,128]{0,1:T(8,128)S(1)} %get-tuple-element.623) | copy-start | bytes 1572868
  12.8 179.7 %copy-start.9 = (f32[1024,128]{0,1:T(8,128)}, f32[1024,128]{0,1:T(8,128)S(1)}, u32[]{:S(2)}) copy-start(f32[1024,128]{0,1:T(8,128)S(1)} %get-tuple-element.624) | copy-start | bytes 1572868
  190.9 3.3 copy-start.21
  197.7 6.5 %slice-start = ((f32[1024,1024]{0,1:T(8,128)}), f32[1024,512]{0,1:T(8,128)S(1)}, s32[]{:S(2)}) async-start(f32[1024,1024]{0,1:T(8,128)} %copy-done.3), calls=%async_computation.13 | async-start | bytes 4194304 | tf_op jit(solution)/shard_map/jvp()/slice | solution.py:57
  207.4 6.1 %copy-start.8 = (bf16[1024,2,128]{2,0,1:T(8,128)(2,1)S(1)}, bf16[1024,2,128]{2,0,1:T(8,128)(2,1)}, u32[]{:S(2)}) copy-start(bf16[1024,2,128]{2,0,1:T(8,128)(2,1)} %copy.93) | copy-start | bytes 1572868
  213.5 49.2 %copy-start.10 = (f32[1024,128]{0,1:T(8,128)S(1)}, f32[1024,128]{0,1:T(8,128)}, u32[]{:S(2)}) copy-start(f32[1024,128]{0,1:T(8,128)} %copy-done.9) | copy-start | bytes 1572868
  214.3 3.5 copy-start.18
  217.9 3.9 copy-start.1
  228.5 4.8 %copy-start.2 = (f32[2,512,2,1024]{3,1,2,0:T(8,128)S(1)}, f32[2,512,2,1024]{3,1,2,0:T(8,128)}, u32[]{:S(2)}) copy-start(f32[2,512,2,1024]{3,1,2,0:T(8,128)} %copy-done.1) | copy-start | bytes 25165828 | tf_op jit(solution)/shard_map/while
  238.8 3.5 copy-start.18
  242.3 3.9 copy-start.1
  252.9 4.8 %copy-start.2 = (f32[2,512,2,1024]{3,1,2,0:T(8,128)S(1)}, f32[2,512,2,1024]{3,1,2,0:T(8,128)}, u32[]{:S(2)}) copy-start(f32[2,512,2,1024]{3,1,2,0:T(8,128)} %copy-done.1) | copy-start | bytes 25165828 | tf_op jit(solution)/shard_map/while
  262.7 2.3 copy-start.7
  262.7 2.3 copy-start.30
  262.7 2.7 copy-start.26
  262.7 2.8 copy-start.24
  269.1 2.3 copy-start.5
  269.1 2.3 copy-start.28
  272.4 2.3 slice-start.2
  272.4 3.2 copy-start.31
  273.4 9.0 %copy-start.13 = (f32[1024,4,128]{0,2,1:T(8,128)}, f32[1024,4,128]{0,2,1:T(8,128)S(1)}, u32[]{:S(2)}) copy-start(f32[1024,4,128]{0,2,1:T(8,128)S(1)} %add_add_fusion) | copy-start | bytes 6291460
  282.4 2.4 copy-start.12
  288.6 66.3 %reduce-scatter.17.cloned.1.call-start = ((), (), s32[]{:S(2)}) async-start(), calls=%async_computation.12 | async-start | bytes 1720320
  290.2 120.1 %reduce-scatter.13.cloned.1.call-start = ((), (), s32[]{:S(2)}) async-start(), calls=%async_computation.10 | async-start | bytes 3440640
  293.9 5.0 %copy-start.14 = (f32[1024,4,128]{0,2,1:T(8,128)S(1)}, f32[1024,4,128]{0,2,1:T(8,128)}, u32[]{:S(2)}) copy-start(f32[1024,4,128]{0,2,1:T(8,128)} %copy-done.13) | copy-start | bytes 6291460
  298.8 173.1 %reduce-scatter.11.cloned.1.call-start = ((), (), s32[]{:S(2)}) async-start(), calls=%async_computation.9 | async-start | bytes 6193152 | tf_op jit(solution)/shard_map/reduce_scatter | solution.py:226
  (15 other events, 27.7 us)
Sparse Core Ops, SparseCore 0:
  9.6 59.6 all-gather.4
  70.9 32.5 all-gather.6
  105.0 32.7 all-gather.8
  139.6 41.1 all-gather.10
  288.8 32.2 reduce-scatter.14
  323.9 31.0 reduce-scatter.16
  357.3 52.9 reduce-scatter.12
  414.4 57.5 reduce-scatter.10
where the time goes:
time: 480 us; the launch traced here: 479 us
  waiting for transfers between devices  275 us (57%)
  matrix products  73.7 us (15%)
  local copies, waits for them, and re-layouts  70 us (15%)
  other arithmetic  25.1 us (5%)
  blocking collectives  18.8 us (4%)
  between operations  14.7 us (3%)
    unnamed x11, waiting for transfers between devices  60.1 us
    reduce_scatter x1, waiting for transfers between devices, local(): lax.psum_scatter(lax.dot_general(projection_gradient, joined, (((1,), (1,...  58.9 us
    all_gather x1, waiting for transfers between devices, local(): lax.all_gather(q_weight, 'dp', axis=0, tiled=True)  53 us
    all_gather x1, waiting for transfers between devices, local(): row_tokens = lax.all_gather(tokens, 'seq', axis=0, tiled=True)  40.3 us
    unnamed x74, local copies, waits for them, and re-layouts  35 us
    all_gather x1, waiting for transfers between devices, local(): lax.all_gather(value_projection, 'dp', axis=0, tiled=True)  31.8 us
    all_gather x1, waiting for transfers between devices, local(): lax.all_gather(key_projection, 'dp', axis=0, tiled=True)  30.6 us
    all_to_all x1, blocking collectives, local(): lax.all_to_all(head_output, 'seq', split_axis=0, concat_axis=1, tiled=True)  18.8 us
  transfers between devices with their start and end apart: 8, of which 7 were waited for; matrix products, arithmetic and copies ran while one was open for 13% of the time, Pallas kernels for 0%

commit v1 on v0

v1 whole, which is shorter than its diff:
```python
import functools

import jax
import jax.numpy as jnp
from jax import lax
from jax.experimental import pallas as pl
from jax.experimental.pallas import tpu as pltpu
from jax.sharding import PartitionSpec as P

HEAD_WIDTH = 128
WINDOW = 1024
QUERY_BLOCK = 256

score_scale = 168.0 ** (-0.5)
rope_base = 10000.0
norm_eps = 1e-06
NN = (((1,), (0,)), ((), ()))
NT = (((1,), (1,)), ((), ()))
TN = (((0,), (0,)), ((), ()))


def dot(a, b, dims):
    return lax.dot_general(a, b, dims, preferred_element_type=jnp.float32)


def doc_tables(length_row, length):
    ends = jnp.cumsum(length_row, dtype=jnp.int32)
    starts = ends - length_row
    token = jnp.arange(length, dtype=jnp.int32)
    inside = (token[:, None] >= starts[None, :]) & (token[:, None] < ends[None, :])
    start = jnp.sum(jnp.where(inside, starts[None, :], 0), axis=1, dtype=jnp.int32)
    half = HEAD_WIDTH // 2
    inverse = rope_base ** (-jnp.arange(half, dtype=jnp.float32) * (2.0 / HEAD_WIDTH))
    angle = (token - start).astype(jnp.float32)[:, None] * inverse[None, :]
    cosine, sine = jnp.cos(angle), jnp.sin(angle)
    first = jnp.maximum(start, token - (WINDOW - 1))
    return (
        jnp.concatenate([cosine, cosine], axis=1),
        jnp.concatenate([-sine, sine], axis=1),
        first[:, None],
    )


def rotate(vectors, gain, cosine, sine):
    factor = lax.rsqrt(jnp.mean(vectors * vectors, axis=1, keepdims=True) + norm_eps)
    normed = vectors * factor * gain
    return normed * cosine + pltpu.roll(normed, HEAD_WIDTH // 2, 1) * sine


def rotate_back(grad, vectors, gain, cosine, sine):
    factor = lax.rsqrt(jnp.mean(vectors * vectors, axis=1, keepdims=True) + norm_eps)
    inner = (grad * cosine + pltpu.roll(grad * sine, HEAD_WIDTH // 2, 1)) * gain
    shared = jnp.mean(inner * vectors, axis=1, keepdims=True) * (factor * factor * factor)
    return inner * factor - vectors * shared


def head_kernel(planes, share, tokens_hbm, *refs):
    pieces = refs[: 2 * planes - 1]
    (cos_ref, sin_ref, first_ref, qgain_ref, kgain_ref, cot_ref) = refs[2 * planes - 1 : 2 * planes + 5]
    out_ref, grad_ref, weight_hbm = refs[2 * planes + 5 : 2 * planes + 8]
    (tok, weight, proj, query, key, value, key_sum, value_sum, piece_sem, tok_sem, weight_sem) = refs[
        2 * planes + 8 :
    ]
    length, rows = tok.shape[0], pieces[0].shape[0]
    blocks = length // QUERY_BLOCK
    mine = lax.axis_index("dp")

    def piece_copy(slot, place):
        at = pl.multiple_of(place * rows, 16)
        return pltpu.make_async_copy(
            pieces[slot], weight.at[pl.ds(at, rows)], piece_sem.at[slot]
        )

    def each_piece(act):
        act(piece_copy(0, mine))
        for step in range(1, planes):

            @pl.when(mine >= step)
            def _():
                act(piece_copy(step, mine - step))

            @pl.when(mine + step < planes)
            def _():
                act(piece_copy(planes - 1 + step, mine + step))

    def tok_copy(block):
        at = pl.ds(block * QUERY_BLOCK, QUERY_BLOCK)
        return pltpu.make_async_copy(tokens_hbm.at[at], tok.at[at], tok_sem.at[block])

    each_piece(lambda copy: copy.start())
    for block in range(blocks):
        tok_copy(block).start()
    each_piece(lambda copy: copy.wait())
    weight_copy = pltpu.make_async_copy(weight, weight_hbm, weight_sem)
    weight_copy.start()

    qgain, kgain = qgain_ref[...], kgain_ref[...]
    key_at, value_at = share * HEAD_WIDTH, (share + 1) * HEAD_WIDTH
    for block in range(blocks):
        tok_copy(block).wait()
        at = pl.ds(block * QUERY_BLOCK, QUERY_BLOCK)
        part = dot(tok[at, :], weight[...], NN)
        proj[at, :] = part
        cosine, sine = cos_ref[at, :], sin_ref[at, :]
        for head in range(share):
            cols = slice(head * HEAD_WIDTH, (head + 1) * HEAD_WIDTH)
            query[at, cols] = rotate(part[:, cols], qgain, cosine, sine).astype(jnp.bfloat16)
        key[at, :] = rotate(part[:, key_at:value_at], kgain, cosine, sine).astype(jnp.bfloat16)
        value[at, :] = part[:, value_at:].astype(jnp.bfloat16)

    key_sum[...] = jnp.zeros_like(key_sum)
    value_sum[...] = jnp.zeros_like(value_sum)
    for block in range(blocks):
        start = block * QUERY_BLOCK
        low = max(0, (start - (WINDOW - 1)) // QUERY_BLOCK * QUERY_BLOCK)
        width = start + QUERY_BLOCK - low
        at, keys_at = pl.ds(start, QUERY_BLOCK), pl.ds(low, width)
        key_token = low + lax.broadcasted_iota(jnp.int32, (QUERY_BLOCK, width), 1)
        query_token = start + lax.broadcasted_iota(jnp.int32, (QUERY_BLOCK, 1), 0)
        allowed = (key_token >= first_ref[at, :]) & (key_token <= query_token)
        key_part, value_part = key[keys_at, :], value[keys_at, :]
        cosine, sine = cos_ref[at, :], sin_ref[at, :]
        for head in range(share):
            cols = slice(head * HEAD_WIDTH, (head + 1) * HEAD_WIDTH)
            query_part, cot_part = query[at, cols], cot_ref[at, cols]
            scores = dot(query_part, key_part, NT) * score_scale
            weights = jnp.where(allowed, jnp.exp(scores), 0.0)
            probs = weights * (1.0 / jnp.sum(weights, axis=1, keepdims=True))
            probs_bf = probs.astype(jnp.bfloat16)
            out_ref[at, cols] = dot(probs_bf, value_part, NN).astype(jnp.bfloat16)
            value_sum[keys_at, :] += dot(probs_bf, cot_part, TN)
            grad_probs = dot(cot_part, value_part, NT)
            delta = jnp.sum(probs * grad_probs, axis=1, keepdims=True)
            grad_scores = (probs * (grad_probs - delta)).astype(jnp.bfloat16)
            key_sum[keys_at, :] += dot(grad_scores, query_part, TN)
            grad_query = dot(grad_scores, key_part, NN) * score_scale
            grad_ref[at, cols] = rotate_back(
                grad_query, proj[at, cols], qgain, cosine, sine
            ).astype(jnp.bfloat16)
    for block in range(blocks):
        at = pl.ds(block * QUERY_BLOCK, QUERY_BLOCK)
        grad_ref[at, key_at:value_at] = rotate_back(
            key_sum[at, :] * score_scale,
            proj[at, key_at:value_at],
            kgain,
            cos_ref[at, :],
            sin_ref[at, :],
        ).astype(jnp.bfloat16)
        grad_ref[at, value_at:] = value_sum[at, :].astype(jnp.bfloat16)
    weight_copy.wait()


def heads(planes, share, row_tokens, pieces, tables, gains, cot):
    length, model = row_tokens.shape
    width = pieces[0].shape[1]
    blocks = length // QUERY_BLOCK
    hbm = pl.BlockSpec(memory_space=pl.ANY)
    vmem = pl.BlockSpec(memory_space=pltpu.VMEM)
    return pl.pallas_call(
        functools.partial(head_kernel, planes, share),
        out_shape=(
            jax.ShapeDtypeStruct((length, share * HEAD_WIDTH), jnp.bfloat16),
            jax.ShapeDtypeStruct((length, width), jnp.bfloat16),
            jax.ShapeDtypeStruct((model, width), jnp.bfloat16),
        ),
        in_specs=[hbm] * (2 * planes) + [vmem] * 6,
        out_specs=(vmem, vmem, hbm),
        scratch_shapes=[
            pltpu.VMEM((length, model), jnp.bfloat16),
            pltpu.VMEM((model, width), jnp.bfloat16),
            pltpu.VMEM((length, width), jnp.float32),
            pltpu.VMEM((length, share * HEAD_WIDTH), jnp.bfloat16),
            pltpu.VMEM((length, HEAD_WIDTH), jnp.bfloat16),
            pltpu.VMEM((length, HEAD_WIDTH), jnp.bfloat16),
            pltpu.VMEM((length, HEAD_WIDTH), jnp.float32),
            pltpu.VMEM((length, HEAD_WIDTH), jnp.float32),
            pltpu.SemaphoreType.DMA((2 * planes - 1,)),
            pltpu.SemaphoreType.DMA((blocks,)),
            pltpu.SemaphoreType.DMA,
        ],
        compiler_params=pltpu.CompilerParams(vmem_limit_bytes=48 * 1024 * 1024),
        cost_estimate=pl.CostEstimate(
            flops=2 * length * model * width + 12 * share * length * length * HEAD_WIDTH,
            bytes_accessed=2 * (length * model + 2 * model * width + 4 * length * width),
            transcendentals=share * length * length,
        ),
        name="heads",
    )(row_tokens, *pieces, *tables, *gains, cot)


def token_kernel(groups, *refs):
    total = None
    for group in range(groups):
        term = dot(refs[group][...], refs[groups + group][...], NT)
        total = term if total is None else total + term
    refs[-1][...] = total.astype(jnp.bfloat16)


def token_terms(grads, weights):
    groups = len(grads)
    length, width = grads[0].shape
    model = weights[0].shape[0]
    return pl.pallas_call(
        functools.partial(token_kernel, groups),
        grid=(length // QUERY_BLOCK,),
        out_shape=jax.ShapeDtypeStruct((length, model), jnp.bfloat16),
        in_specs=[pl.BlockSpec((QUERY_BLOCK, width), lambda i: (i, 0))] * groups
        + [pl.BlockSpec((model, width), lambda i: (0, 0))] * groups,
        out_specs=pl.BlockSpec((QUERY_BLOCK, model), lambda i: (i, 0)),
        compiler_params=pltpu.CompilerParams(vmem_limit_bytes=48 * 1024 * 1024),
        cost_estimate=pl.CostEstimate(
            flops=2 * length * model * width * groups,
            bytes_accessed=2 * (length * model + groups * width * (length + model)),
            transcendentals=0,
        ),
        name="token_terms",
    )(*grads, *weights)


def gather_line(block, planes):
    left, right, from_left, from_right = block, block, [], []
    for step in range(1, planes):
        left = lax.ppermute(left, "dp", [(i, i + 1) for i in range(step - 1, planes - 1)])
        right = lax.ppermute(right, "dp", [(i, i - 1) for i in range(1, planes - step + 1)])
        from_left.append(left)
        from_right.append(right)
    return [block] + from_left + from_right


def local(planes, tokens, q_weight, key_projection, value_projection, q_gain, k_gain, doc_lengths, out_cot):
    value_heads = key_projection.shape[1] // HEAD_WIDTH
    share = q_weight.shape[1] // key_projection.shape[1]
    wide = share * HEAD_WIDTH
    row_tokens = lax.all_gather(tokens, "seq", axis=0, tiled=True)
    tables = doc_tables(doc_lengths[0], row_tokens.shape[0])
    gains = (q_gain[None, :], k_gain[None, :])
    outs, grads, weights, sums = [], [], [], []
    for group in range(value_heads):
        narrow = slice(group * HEAD_WIDTH, (group + 1) * HEAD_WIDTH)
        broad = slice(group * wide, (group + 1) * wide)
        block = jnp.concatenate(
            [q_weight[:, broad], key_projection[:, narrow], value_projection[:, narrow]], axis=1
        )
        out, grad, weight = heads(
            planes, share, row_tokens, gather_line(block, planes), tables, gains, out_cot[:, broad]
        )
        outs.append(out)
        grads.append(grad)
        weights.append(weight)
        sums.append(
            lax.psum_scatter(
                dot(row_tokens, grad, TN).astype(jnp.bfloat16), "dp", scatter_dimension=0, tiled=True
            )
        )
    attn_out = lax.all_to_all(
        jnp.concatenate(outs, axis=1), "seq", split_axis=0, concat_axis=1, tiled=True
    )
    token_grad = lax.psum_scatter(
        token_terms(grads, weights), "seq", scatter_dimension=0, tiled=True
    )

    def columns(first, count):
        return jnp.concatenate(
            [s[:, first : first + count].astype(jnp.float32) for s in sums], axis=1
        )

    return (
        attn_out,
        token_grad,
        columns(0, wide),
        columns(wide, HEAD_WIDTH),
        columns(wide + HEAD_WIDTH, HEAD_WIDTH),
    )


def solution(mesh):
    rows, split = P(("dp", "seq"), None), P("dp", "seq")
    return jax.shard_map(
        functools.partial(local, mesh.shape["dp"]),
        mesh=mesh,
        in_specs=(rows, split, split, split, P(), P(), P("dp", None), split),
        out_specs=(rows, rows, split, split, split),
        check_vma=False,
    )
```

time: 480 us -> 350 us (0.73)
  waiting for transfers between devices: 275 us -> 201 us
  matrix products: 73.7 us -> 12.6 us
  Pallas kernels: 0 us -> 46.3 us
  local copies, waits for them, and re-layouts: 70 us -> 32 us
  other arithmetic: 25.1 us -> 5.4 us
  starting transfers between devices: 0.31 us -> 18.9 us
    ppermute x0 -> x12, waiting for transfers between devices: none -> 129 us  [the longest x6 89.6 us: gather_line(): lax.ppermute(right, 'dp', [(i, i - 1) for i in range(1, planes - step + 1)])]
    all_gather x3 -> x0, waiting for transfers between devices: 115 us -> none  [the longest x1 53 us: local(): lax.all_gather(q_weight, 'dp', axis=0, tiled=True)]
    dot_general x17 -> x2, matrix products: 73.7 us -> 12.6 us  [dot(): return lax.dot_general(a, b, dims, preferred_element_type=jnp.float32)]
    pallas_call x0 -> x3, Pallas kernels: none -> 46.3 us  [the longest x2 36.6 us: heads(): pl.pallas_call(functools.partial(head_kernel, planes, share), out_shape=(...]
    unnamed x11 -> x6, waiting for transfers between devices: 60.1 us -> 17.8 us
    all_gather x1, waiting for transfers between devices: 40.3 us -> 0.01 us  [local(): row_tokens = lax.all_gather(tokens, 'seq', axis=0, tiled=True)]
    ppermute x0 -> x12, starting transfers between devices: none -> 18.7 us  [the longest x6 11 us: gather_line(): lax.ppermute(left, 'dp', [(i, i + 1) for i in range(step - 1, planes - 1)])]
    unnamed x74 -> x57, local copies, waits for them, and re-layouts: 35 us -> 23.3 us
  transfers between devices with their start and end apart: 8 -> 16, of which waited for: 7 -> 10; matrix products, arithmetic and copies ran while one was open for 13% -> 9% of each run, Pallas kernels for 0% -> 8%
where the time goes in v1:
time: 350 us; the launch traced here: 349 us
  waiting for transfers between devices  201 us (57%)
  Pallas kernels  46.3 us (13%)
  local copies, waits for them, and re-layouts  32 us (9%)
  starting transfers between devices  18.9 us (5%)
  blocking collectives  18.6 us (5%)
  between operations  14.1 us (4%)
  matrix products  12.6 us (4%)
  other arithmetic  5.4 us (2%)
    ppermute x6, waiting for transfers between devices, gather_line(): lax.ppermute(right, 'dp', [(i, i - 1) for i in range(1, planes - step + 1)])  89.6 us
    reduce_scatter x1, waiting for transfers between devices, local(): lax.psum_scatter(token_terms(grads, weights), 'seq', scatter_dimension=0,...  54.7 us
    ppermute x6, waiting for transfers between devices, gather_line(): lax.ppermute(left, 'dp', [(i, i + 1) for i in range(step - 1, planes - 1)])  38.9 us
    pallas_call x2, Pallas kernels, heads(): pl.pallas_call(functools.partial(head_kernel, planes, share), out_shape=(...  36.6 us
    unnamed x57, local copies, waits for them, and re-layouts  23.3 us
    all_to_all x1, blocking collectives, local(): lax.all_to_all(jnp.concatenate(outs, axis=1), 'seq', split_axis=0, concat...  18.6 us
    unnamed x6, waiting for transfers between devices  17.8 us
    dot_general x2, matrix products, dot(): return lax.dot_general(a, b, dims, preferred_element_type=jnp.float32)  12.6 us
  transfers between devices with their start and end apart: 16, of which 10 were waited for; matrix products, arithmetic and copies ran while one was open for 9% of the time, Pallas kernels for 8%

profile of v1, /device:TPU:0, one launch (start us, length us, event | category | flops | bytes accessed | tf_op | source)
XLA Modules:
  0.0 349.0 jit_solution(5974966290604025648)
XLA Ops:
  8.0 1.9 fusion.8
  10.7 5.0 %collective-permute-start.6 = (bf16[672,512]{1,0:T(8,128)(2,1)S(1)}, bf16[672,512]{1,0:T(8,128)(2,1)S(1)}, u32[]{:S(2)}, u32[]{:S(2)}) collective-permute-start(bf16[672,512]{1,0:T(8,128)(2,1)S(1)} %pad_maximum_fusion.2.refs_0_), channel_id=1, source_target_pairs={{0,8},{8,16},{16,24},{1,9},{9,17},{17,25},{2,10},{10,18},{18,26},{... | collective-permute-start | bytes 2064392 | tf_op jit(solution)/shard_map/ppermute | solution.py:223
  15.7 1.3 collective-permute-start.9
  17.0 13.3 %collective-permute-done.6.refs_1_ = bf16[672,512]{1,0:T(8,128)(2,1)S(1)} collective-permute-done((bf16[672,512]{1,0:T(8,128)(2,1)S(1)}, bf16[672,512]{1,0:T(8,128)(2,1)S(1)}, u32[]{:S(2)}, u32[]{:S(2)}) %collective-permute-start.6) | collective-permute-done | bytes 688160 | tf_op jit(solution)/shard_map/ppermute | solution.py:223
  30.3 1.5 collective-permute-start.7
  31.8 2.6 collective-permute-done.9.refs_4_
  34.5 1.3 collective-permute-start.10
  36.1 1.5 collective-permute-start.8
  37.6 16.0 %collective-permute-done.10.refs_5_ = bf16[672,512]{1,0:T(8,128)(2,1)} collective-permute-done((bf16[672,512]{1,0:T(8,128)(2,1)S(1)}, bf16[672,512]{1,0:T(8,128)(2,1)}, u32[]{:S(2)}, u32[]{:S(2)}) %collective-permute-start.10) | collective-permute-done | bytes 688160 | tf_op jit(solution)/shard_map/ppermute | solution.py:224
  53.5 1.3 collective-permute-start.11
  54.8 3.0 fusion.2
  58.8 1.7 pad_maximum_fusion.3
  61.5 9.7 %collective-permute-done.11.refs_6_ = bf16[672,512]{1,0:T(8,128)(2,1)} collective-permute-done((bf16[672,512]{1,0:T(8,128)(2,1)}, bf16[672,512]{1,0:T(8,128)(2,1)}, u32[]{:S(2)}, u32[]{:S(2)}) %collective-permute-start.11) | collective-permute-done | bytes 688160 | tf_op jit(solution)/shard_map/ppermute | solution.py:224
  74.5 18.6 %heads.3 = (bf16[1024,256]{1,0:T(8,128)(2,1)S(1)}, bf16[1024,512]{1,0:T(8,128)(2,1)}, bf16[2688,512]{1,0:T(8,128)(2,1)}) custom-call(bf16[1024,2688]{1,0:T(8,128)(2,1)} %all-gather.2.cloned.1.call-done.tokens_hbm, bf16[672,512]{1,0:T(8,128)(2,1)S(1)} %pad_maximum_fusion.2.refs_0_, bf16[672,512]{1,0:T(8,128)(2,1)S(1)} %copy-done.2, ...), custom_call_target="tpu_custom_call" | custom-call | flops 6039797760 | bytes 15204352 | tf_op jit(solution)/shard_map/heads/pallas_call | solution.py:159
  93.0 6.3 %fusion.1 = bf16[2688,512]{0,1:T(8,128)(2,1)} fusion(bf16[1024,512]{1,0:T(8,128)(2,1)} %get-tuple-element.14.refs_1_, bf16[1024,2688]{1,0:T(8,128)(2,1)S(1)} %copy-done.17), kind=kOutput, calls=%fused_computation.3 | convolution fusion | flops 2819948544 | bytes 9306112 | tf_op jit(solution)/shard_map/dot_general | solution.py:23
  99.3 4.6 %copy.34 = bf16[2688,512]{1,0:T(8,128)(2,1)} copy(bf16[2688,512]{0,1:T(8,128)(2,1)} %fusion.1) | data formatting | bytes 5505024
  105.0 1.6 collective-permute-start
  106.6 1.3 collective-permute-start.3
  107.9 25.5 %collective-permute-done.refs_1_ = bf16[672,512]{1,0:T(8,128)(2,1)S(1)} collective-permute-done((bf16[672,512]{1,0:T(8,128)(2,1)S(1)}, bf16[672,512]{1,0:T(8,128)(2,1)S(1)}, u32[]{:S(2)}, u32[]{:S(2)}) %collective-permute-start) | collective-permute-done | bytes 688160 | tf_op jit(solution)/shard_map/ppermute | solution.py:223
  134.2 24.9 %collective-permute-done.3.refs_4_ = bf16[672,512]{1,0:T(8,128)(2,1)S(1)} collective-permute-done((bf16[672,512]{1,0:T(8,128)(2,1)S(1)}, bf16[672,512]{1,0:T(8,128)(2,1)S(1)}, u32[]{:S(2)}, u32[]{:S(2)}) %collective-permute-start.3) | collective-permute-done | bytes 688160 | tf_op jit(solution)/shard_map/ppermute | solution.py:224
  161.1 20.9 %collective-permute-done.4.refs_5_ = bf16[672,512]{1,0:T(8,128)(2,1)S(1)} collective-permute-done((bf16[672,512]{1,0:T(8,128)(2,1)S(1)}, bf16[672,512]{1,0:T(8,128)(2,1)S(1)}, u32[]{:S(2)}, u32[]{:S(2)}) %collective-permute-start.4) | collective-permute-done | bytes 688160 | tf_op jit(solution)/shard_map/ppermute | solution.py:224
  182.1 1.3 collective-permute-start.5
  183.4 15.4 %collective-permute-done.5.refs_6_ = bf16[672,512]{1,0:T(8,128)(2,1)S(1)} collective-permute-done((bf16[672,512]{1,0:T(8,128)(2,1)S(1)}, bf16[672,512]{1,0:T(8,128)(2,1)S(1)}, u32[]{:S(2)}, u32[]{:S(2)}) %collective-permute-start.5) | collective-permute-done | bytes 688160 | tf_op jit(solution)/shard_map/ppermute | solution.py:224
  199.7 18.1 %heads.2 = (bf16[1024,256]{1,0:T(8,128)(2,1)S(1)}, bf16[1024,512]{1,0:T(8,128)(2,1)}, bf16[2688,512]{1,0:T(8,128)(2,1)}) custom-call(bf16[1024,2688]{1,0:T(8,128)(2,1)} %all-gather.2.cloned.1.call-done.tokens_hbm, bf16[672,512]{1,0:T(8,128)(2,1)S(1)} %pad_maximum_fusion.1.refs_0_, bf16[672,512]{1,0:T(8,128)(2,1)S(1)} %collective-permute-done.refs_1_, ...), custom_call_target="tpu_custom_call" | custom-call | flops 6039797760 | bytes 15204352 | tf_op jit(solution)/shard_map/heads/pallas_call | solution.py:159
  217.8 6.3 %fusion = bf16[2688,512]{0,1:T(8,128)(2,1)} fusion(bf16[1024,512]{1,0:T(8,128)(2,1)} %get-tuple-element.13.refs_0_, bf16[1024,2688]{1,0:T(8,128)(2,1)S(1)} %bitcast.35), kind=kOutput, calls=%fused_computation.2 | convolution fusion | flops 2819948544 | bytes 9306112 | tf_op jit(solution)/shard_map/dot_general | solution.py:23
  224.1 4.6 %copy.32 = bf16[2688,512]{1,0:T(8,128)(2,1)} copy(bf16[2688,512]{0,1:T(8,128)(2,1)} %fusion) | data formatting | bytes 5505024
  231.2 2.0 copy-done.9
  233.1 9.7 %token_terms.1 = bf16[1024,2688]{1,0:T(8,128)(2,1)} custom-call(bf16[1024,512]{1,0:T(8,128)(2,1)S(1)} %copy-done.8, bf16[1024,512]{1,0:T(8,128)(2,1)S(1)} %copy-done.7, bf16[2688,512]{1,0:T(8,128)(2,1)S(1)} %copy-done.9, bf16[2688,512]{1,0:T(8,128)(2,1)} %get-tuple-element.16.refs_3_), custom_call_target="tpu_custom_call" | custom-call | flops 5637144576 | bytes 13107200 | tf_op jit(solution)/shard_map/token_terms/pallas_call | solution.py:203
  243.0 18.6 %all_to_all.19 = bf16[8,128,512]{2,1,0:T(8,128)(2,1)S(1)} all-to-all(bf16[8,128,512]{2,1,0:T(8,128)(2,1)S(1)} %bitcast.29), channel_id=1, replica_groups=mesh['dp'=4,'seq'=8] {'seq'}, dimensions={0} | all-to-all | bytes 2097152 | tf_op jit(solution)/shard_map/all_to_all | solution.py:255
  263.9 17.1 %reduce-scatter.10.cloned.1.call-done = bf16[672,512]{1,0:T(8,128)(2,1)} async-done(((bf16[2688,512]{1,0:T(8,128)(2,1)}), bf16[672,512]{1,0:T(8,128)(2,1)}) %reduce-scatter.10.cloned.1.call-update) | async-done | bytes 688144
  282.3 1.5 copy.29
  287.8 54.7 %reduce-scatter.8.cloned.1.call-done = bf16[128,2688]{1,0:T(8,128)(2,1)} async-done(((bf16[1024,2688]{1,0:T(8,128)(2,1)}), bf16[128,2688]{1,0:T(8,128)(2,1)}) %reduce-scatter.8.cloned.1.call-update) | async-done | bytes 688144 | tf_op jit(solution)/shard_map/reduce_scatter | solution.py:258
  (91 shorter events, 21.8 us)
Async XLA Ops:
  7.2 2.7 copy-start.15
  7.2 2.7 copy-start.16
  7.2 64.0 %all-gather.2.cloned.1.call-start = ((), (), s32[]{:S(2)}) async-start(), calls=%async_computation.4 | async-start | bytes 6193152 | tf_op jit(solution)/shard_map/all_gather | solution.py:234
  7.9 27.8 %copy-start.20 = (s32[1,4]{1,0:T(1,128)S(1)}, s32[1,4]{1,0:T(1,128)}, u32[]{:S(2)}) copy-start(s32[1,4]{1,0:T(1,128)} %param.14) | copy-start | bytes 52
  7.9 254.8 %reduce-scatter.12.cloned.1.call-start = ((), (), s32[]{:S(2)}) async-start(), calls=%async_computation.7 | async-start | bytes 3440640
  10.7 19.6 %collective-permute-start.6 = (bf16[672,512]{1,0:T(8,128)(2,1)S(1)}, bf16[672,512]{1,0:T(8,128)(2,1)S(1)}, u32[]{:S(2)}, u32[]{:S(2)}) collective-permute-start(bf16[672,512]{1,0:T(8,128)(2,1)S(1)} %pad_maximum_fusion.2.refs_0_), channel_id=1, source_target_pairs={{0,8},{8,16},{16,24},{1,9},{9,17},{17,25},{2,10},{10,18},{18,26},{... | collective-permute-start | bytes 2064392 | tf_op jit(solution)/shard_map/ppermute | solution.py:223
  15.7 18.8 %collective-permute-start.9 = (bf16[672,512]{1,0:T(8,128)(2,1)S(1)}, bf16[672,512]{1,0:T(8,128)(2,1)S(1)}, u32[]{:S(2)}, u32[]{:S(2)}) collective-permute-start(bf16[672,512]{1,0:T(8,128)(2,1)S(1)} %pad_maximum_fusion.2.refs_0_), channel_id=1, source_target_pairs={{8,0},{16,8},{24,16},{9,1},{17,9},{25,17},{10,2},{18,10},{26,18},{... | collective-permute-start | bytes 2064392 | tf_op jit(solution)/shard_map/ppermute | solution.py:224
  30.3 28.5 %copy-start.1 = (bf16[672,512]{1,0:T(8,128)(2,1)}, bf16[672,512]{1,0:T(8,128)(2,1)S(1)}, u32[]{:S(2)}) copy-start(bf16[672,512]{1,0:T(8,128)(2,1)S(1)} %collective-permute-done.6.refs_1_) | copy-start | bytes 2064388
  30.3 5.8 %collective-permute-start.7 = (bf16[672,512]{1,0:T(8,128)(2,1)S(1)}, bf16[672,512]{1,0:T(8,128)(2,1)}, u32[]{:S(2)}, u32[]{:S(2)}) collective-permute-start(bf16[672,512]{1,0:T(8,128)(2,1)S(1)} %collective-permute-done.6.refs_1_), channel_id=1, source_target_pairs={{8,16},{16,24},{9,17},{17,25},{10,18},{18,26},{11,19},{19,27},{12,... | collective-permute-start | bytes 2064392 | tf_op jit(solution)/shard_map/ppermute | solution.py:223
  34.5 24.4 %copy-start.3 = (bf16[672,512]{1,0:T(8,128)(2,1)}, bf16[672,512]{1,0:T(8,128)(2,1)S(1)}, u32[]{:S(2)}) copy-start(bf16[672,512]{1,0:T(8,128)(2,1)S(1)} %collective-permute-done.9.refs_4_) | copy-start | bytes 2064388
  34.5 19.1 %collective-permute-start.10 = (bf16[672,512]{1,0:T(8,128)(2,1)S(1)}, bf16[672,512]{1,0:T(8,128)(2,1)}, u32[]{:S(2)}, u32[]{:S(2)}) collective-permute-start(bf16[672,512]{1,0:T(8,128)(2,1)S(1)} %collective-permute-done.9.refs_4_), channel_id=1, source_target_pairs={{8,0},{16,8},{9,1},{17,9},{10,2},{18,10},{11,3},{19,11},{12,4},{20... | collective-permute-start | bytes 2064392 | tf_op jit(solution)/shard_map/ppermute | solution.py:224
  36.1 25.4 %collective-permute-start.8 = (bf16[672,512]{1,0:T(8,128)(2,1)}, bf16[672,512]{1,0:T(8,128)(2,1)}, u32[]{:S(2)}, u32[]{:S(2)}) collective-permute-start(bf16[672,512]{1,0:T(8,128)(2,1)} %collective-permute-done.7.refs_2_), channel_id=1, source_target_pairs={{16,24},{17,25},{18,26},{19,27},{20,28},{21,29},{22,30},{23,31}} | collective-permute-start | bytes 2064392 | tf_op jit(solution)/shard_map/ppermute | solution.py:223
  53.5 17.7 %collective-permute-start.11 = (bf16[672,512]{1,0:T(8,128)(2,1)}, bf16[672,512]{1,0:T(8,128)(2,1)}, u32[]{:S(2)}, u32[]{:S(2)}) collective-permute-start(bf16[672,512]{1,0:T(8,128)(2,1)} %collective-permute-done.10.refs_5_), channel_id=1, source_target_pairs={{8,0},{9,1},{10,2},{11,3},{12,4},{13,5},{14,6},{15,7}} | collective-permute-start | bytes 2064392 | tf_op jit(solution)/shard_map/ppermute | solution.py:224
  58.8 1.7 copy-start.10
  58.8 1.8 copy-start.12
  60.5 10.7 %copy-start.5 = (f32[128]{0:T(128)S(1)}, f32[128]{0:T(128)}, u32[]{:S(2)}) copy-start(f32[128]{0:T(128)} %param.12) | copy-start | bytes 1540
  60.5 10.7 %copy-start.6 = (f32[128]{0:T(128)S(1)}, f32[128]{0:T(128)}, u32[]{:S(2)}) copy-start(f32[128]{0:T(128)} %param.13) | copy-start | bytes 1540
  74.5 18.6 %copy-start.17 = (bf16[1024,2688]{1,0:T(8,128)(2,1)S(1)}, bf16[1024,2688]{1,0:T(8,128)(2,1)}, u32[]{:S(2)}) copy-start(bf16[1024,2688]{1,0:T(8,128)(2,1)} %all-gather.2.cloned.1.call-done.tokens_hbm) | copy-start | bytes 16515076
  104.0 177.0 %reduce-scatter.10.cloned.1.call-start = ((), (), s32[]{:S(2)}) async-start(), calls=%async_computation.6 | async-start | bytes 3440640
  104.9 112.8 %slice-start = ((s8[5505024]{0:T(1024)(128)(4,1)}), s8[4194304]{0:T(1024)(128)(4,1)S(1)}, s32[]{:S(2)}) async-start(s8[5505024]{0:T(1024)(128)(4,1)} %bitcast.34), calls=%async_computation.8 | async-start | bytes 8388608
  105.0 28.4 %collective-permute-start = (bf16[672,512]{1,0:T(8,128)(2,1)S(1)}, bf16[672,512]{1,0:T(8,128)(2,1)S(1)}, u32[]{:S(2)}, u32[]{:S(2)}) collective-permute-start(bf16[672,512]{1,0:T(8,128)(2,1)S(1)} %pad_maximum_fusion.1.refs_0_), channel_id=1, source_target_pairs={{0,8},{8,16},{16,24},{1,9},{9,17},{17,25},{2,10},{10,18},{18,26},{... | collective-permute-start | bytes 2064392 | tf_op jit(solution)/shard_map/ppermute | solution.py:223
  106.6 52.5 %collective-permute-start.3 = (bf16[672,512]{1,0:T(8,128)(2,1)S(1)}, bf16[672,512]{1,0:T(8,128)(2,1)S(1)}, u32[]{:S(2)}, u32[]{:S(2)}) collective-permute-start(bf16[672,512]{1,0:T(8,128)(2,1)S(1)} %pad_maximum_fusion.1.refs_0_), channel_id=1, source_target_pairs={{8,0},{16,8},{24,16},{9,1},{17,9},{25,17},{10,2},{18,10},{26,18},{... | collective-permute-start | bytes 2064392 | tf_op jit(solution)/shard_map/ppermute | solution.py:224
  133.5 26.9 %collective-permute-start.1 = (bf16[672,512]{1,0:T(8,128)(2,1)S(1)}, bf16[672,512]{1,0:T(8,128)(2,1)S(1)}, u32[]{:S(2)}, u32[]{:S(2)}) collective-permute-start(bf16[672,512]{1,0:T(8,128)(2,1)S(1)} %collective-permute-done.refs_1_), channel_id=1, source_target_pairs={{8,16},{16,24},{9,17},{17,25},{10,18},{18,26},{11,19},{19,27},{12,... | collective-permute-start | bytes 2064392 | tf_op jit(solution)/shard_map/ppermute | solution.py:223
  159.1 23.0 %collective-permute-start.4 = (bf16[672,512]{1,0:T(8,128)(2,1)S(1)}, bf16[672,512]{1,0:T(8,128)(2,1)S(1)}, u32[]{:S(2)}, u32[]{:S(2)}) collective-permute-start(bf16[672,512]{1,0:T(8,128)(2,1)S(1)} %collective-permute-done.3.refs_4_), channel_id=1, source_target_pairs={{8,0},{16,8},{9,1},{17,9},{10,2},{18,10},{11,3},{19,11},{12,4},{20... | collective-permute-start | bytes 2064392 | tf_op jit(solution)/shard_map/ppermute | solution.py:224
  160.4 22.9 %collective-permute-start.2 = (bf16[672,512]{1,0:T(8,128)(2,1)S(1)}, bf16[672,512]{1,0:T(8,128)(2,1)S(1)}, u32[]{:S(2)}, u32[]{:S(2)}) collective-permute-start(bf16[672,512]{1,0:T(8,128)(2,1)S(1)} %collective-permute-done.1.refs_2_), channel_id=1, source_target_pairs={{16,24},{17,25},{18,26},{19,27},{20,28},{21,29},{22,30},{23,31}} | collective-permute-start | bytes 2064392 | tf_op jit(solution)/shard_map/ppermute | solution.py:223
  182.1 16.7 %copy-start.18 = (bf16[672,512]{1,0:T(8,128)(2,1)}, bf16[672,512]{1,0:T(8,128)(2,1)S(1)}, u32[]{:S(2)}) copy-start(bf16[672,512]{1,0:T(8,128)(2,1)S(1)} %collective-permute-done.4.refs_5_) | copy-start | bytes 2064388
  182.1 16.7 %collective-permute-start.5 = (bf16[672,512]{1,0:T(8,128)(2,1)S(1)}, bf16[672,512]{1,0:T(8,128)(2,1)S(1)}, u32[]{:S(2)}, u32[]{:S(2)}) collective-permute-start(bf16[672,512]{1,0:T(8,128)(2,1)S(1)} %collective-permute-done.4.refs_5_), channel_id=1, source_target_pairs={{8,0},{9,1},{10,2},{11,3},{12,4},{13,5},{14,6},{15,7}} | collective-permute-start | bytes 2064392 | tf_op jit(solution)/shard_map/ppermute | solution.py:224
  199.6 18.1 %slice-start.1 = ((s8[5505024]{0:T(1024)(128)(4,1)}), s8[1310720]{0:T(1024)(128)(4,1)S(1)}, s32[]{:S(2)}) async-start(s8[5505024]{0:T(1024)(128)(4,1)} %bitcast.34), calls=%async_computation.9 | async-start | bytes 2621440
  228.7 1.2 copy-start.7
  228.8 113.7 %reduce-scatter.8.cloned.1.call-start = ((), (), s32[]{:S(2)}) async-start(), calls=%async_computation.5 | async-start | bytes 6193152 | tf_op jit(solution)/shard_map/reduce_scatter | solution.py:258
  231.2 2.0 copy-start.9
  282.2 1.7 copy-start.13
  (7 other events, 7.3 us)
Sparse Core Ops, SparseCore 0:
  9.9 44.9 all-gather.1
  104.1 71.1 reduce-scatter.11
  228.9 52.0 reduce-scatter.9
  284.9 57.5 reduce-scatter.7
